TPU v7x, 32 devices: a whole 2x2x4 slice. The times are simulated.
32 devices in a mesh: row: 4 (over y, x), col: 8 (over z, core).
Axes of the slice: x: 2, y: 2, z: 4, core: 2. Of those that a mesh axis runs over, the one named last changes fastest.
Arguments:
- embeddings: bfloat16 [16384, 768], P(('row', 'col'))
- counts: int32 [32], replicated, may hold values from 256 to 512
- pairs: int32 [32, 6], replicated, may hold values from 0 to 31, as said below
Outputs:
- density: float32 [16384], P(('row', 'col'))
- neighbour: bfloat16 [16384, 768], P(('row', 'col'))
Inputs may be any that keep to these rules, and one draw needn't show every extreme that they name: Row b of pairs lists 6 different blocks; the first is b itself, each other is (b + o) mod 32 for an offset o with 1 <= |o| <= 4; some row lists the offset 4 and some row the offset minus 4.
All inputs are finite; a program needn't handle non-finite values.
Results may differ from a plain program's by a relative error of at most 0.0023.
Values may be sent and summed in bfloat16 or wider, within the bound.
A program may use at most 64 MiB of HBM per device.

v0:
```python
import jax
import jax.numpy as jnp
from jax import lax
from jax.sharding import PartitionSpec as P

REACH = 4


smoothing_scale = 4.0
epsilon = 1e-06


def passed_along(block, axis, distance):
    devices = range(lax.axis_size(axis))
    route = [((i - distance) % len(devices), i) for i in devices]
    return lax.ppermute(block, axis, route)


def reciprocal_norms(block):
    values = block.astype(jnp.float32)
    return lax.rsqrt(jnp.sum(values * values, axis=1) + epsilon)


def body(embeddings, counts, pairs):
    rows_dev, width = embeddings.shape
    row_total = lax.axis_size("row")
    col_total = lax.axis_size("col")
    col_pos = lax.axis_index("col")
    block_id = lax.axis_index("row") * col_total + col_pos
    block_total = row_total * col_total
    own_inverse = reciprocal_norms(embeddings)
    slot_index = jnp.arange(rows_dev, dtype=jnp.int32)
    own_list = lax.dynamic_index_in_dim(pairs, block_id, 0, keepdims=False)

    def add_tile(current, arrived, source):
        is_listed = jnp.any(own_list == source)
        column_count = lax.dynamic_index_in_dim(counts, source, 0, keepdims=False)
        column_valid = slot_index < column_count

        def tile_work(carried):
            total, summed = carried
            products = lax.dot_general(
                embeddings, arrived, (((1,), (1,)), ((), ())), preferred_element_type=jnp.float32
            )
            angular_agreement = products * own_inverse[:, None] * reciprocal_norms(arrived)[None, :]
            eligible_couplings = column_valid[None, :] & is_listed
            coupling_factor = jnp.where(
                eligible_couplings, jnp.exp(smoothing_scale * (angular_agreement - 1.0)), 0.0
            )
            added = jnp.dot(
                coupling_factor.astype(jnp.bfloat16), arrived, preferred_element_type=jnp.float32
            )
            return (total + jnp.sum(coupling_factor, axis=1), summed + added)

        return lax.cond(is_listed, tile_work, lambda carried: carried, current)

    start = (jnp.zeros((rows_dev,), jnp.float32), jnp.zeros((rows_dev, width), jnp.float32))
    running = add_tile(start, embeddings, block_id)
    forward_carry = embeddings
    backward_carry = embeddings
    for distance in range(1, REACH + 1):
        advance_moved = passed_along(forward_carry, ("row", "col"), 1)
        forward_carry = advance_moved
        moved = passed_along(backward_carry, ("row", "col"), -1)
        backward_carry = moved
        running = add_tile(
            running, advance_moved, (block_id - distance + block_total) % block_total
        )
        running = add_tile(running, moved, (block_id + distance) % block_total)
    total, summed = running
    own_count = lax.dynamic_index_in_dim(counts, block_id, 0, keepdims=False)
    own_row_valid = slot_index < own_count
    density = jnp.where(own_row_valid, total, 0.0)
    neighbour = jnp.where(own_row_valid[:, None], summed / total[:, None], 0.0).astype(jnp.bfloat16)
    return (density, neighbour)


def solution(mesh):
    in_specs = (P(("row", "col"), None), P(), P())
    out_specs = (P(("row", "col")), P(("row", "col"), None))
    return jax.shard_map(body, mesh=mesh, in_specs=in_specs, out_specs=out_specs, check_vma=False)
```

profile of v0, /device:TPU:0, one launch (start us, length us, event | category | flops | bytes accessed | tf_op | source)
XLA Modules:
  0.0 111.4 jit_solution(16526270756118755413)
XLA Ops:
  0.6 0.5 collective-permute-start
  1.1 6.0 %collective-permute-start.1 = (bf16[512,768]{1,0:T(8,128)(2,1)}, bf16[512,768]{1,0:T(8,128)(2,1)S(1)}, u32[]{:S(2)}, u32[]{:S(2)}) collective-permute-start(bf16[512,768]{1,0:T(8,128)(2,1)} %param.21), channel_id=1, source_target_pairs={{1,0},{2,1},{3,2},{4,3},{5,4},{6,5},{7,6},{8,7},{9,8},{10,9},{11,1... | collective-permute-start | bytes 2359304 | tf_op jit(solution)/shard_map/ppermute | solution.py:16
  7.1 15.6 %collective-permute-done = bf16[512,768]{1,0:T(8,128)(2,1)S(1)} collective-permute-done((bf16[512,768]{1,0:T(8,128)(2,1)}, bf16[512,768]{1,0:T(8,128)(2,1)S(1)}, u32[]{:S(2)}, u32[]{:S(2)}) %collective-permute-start) | collective-permute-done | bytes 786464 | tf_op jit(solution)/shard_map/ppermute | solution.py:16
  22.7 0.0 collective-permute-start.2
  22.7 0.0 collective-permute-done.1
  22.7 5.3 %collective-permute-start.3 = (bf16[512,768]{1,0:T(8,128)(2,1)S(1)}, bf16[512,768]{1,0:T(8,128)(2,1)S(1)}, u32[]{:S(2)}, u32[]{:S(2)}) collective-permute-start(bf16[512,768]{1,0:T(8,128)(2,1)S(1)} %collective-permute-done.1), channel_id=1, source_target_pairs={{1,0},{2,1},{3,2},{4,3},{5,4},{6,5},{7,6},{8,7},{9,8},{10,9},{11,1... | collective-permute-start | bytes 2359304 | tf_op jit(solution)/shard_map/ppermute | solution.py:16
  28.1 16.7 %collective-permute-done.2 = bf16[512,768]{1,0:T(8,128)(2,1)S(1)} collective-permute-done((bf16[512,768]{1,0:T(8,128)(2,1)S(1)}, bf16[512,768]{1,0:T(8,128)(2,1)S(1)}, u32[]{:S(2)}, u32[]{:S(2)}) %collective-permute-start.2) | collective-permute-done | bytes 786464 | tf_op jit(solution)/shard_map/ppermute | solution.py:16
  44.8 0.0 collective-permute-start.4
  44.8 0.0 collective-permute-done.3
  44.8 0.0 copy-done.3
  44.8 5.3 %collective-permute-start.5 = (bf16[512,768]{1,0:T(8,128)(2,1)S(1)}, bf16[512,768]{1,0:T(8,128)(2,1)}, u32[]{:S(2)}, u32[]{:S(2)}) collective-permute-start(bf16[512,768]{1,0:T(8,128)(2,1)S(1)} %collective-permute-done.3), channel_id=1, source_target_pairs={{1,0},{2,1},{3,2},{4,3},{5,4},{6,5},{7,6},{8,7},{9,8},{10,9},{11,1... | collective-permute-start | bytes 2359304 | tf_op jit(solution)/shard_map/ppermute | solution.py:16
  50.1 1.6 %compare_reduce_fusion = (pred[]{:T(512)}, pred[]{:T(512)}, pred[]{:T(512)}, pred[]{:T(512)}, pred[]{:T(512)}, /*index=5*/pred[]{:T(512)}, pred[]{:T(512)}, pred[]{:T(512)}, pred[]{:T(512)}) fusion(s32[]{:T(128)S(6)} %add.218, s32[32,6]{0,1:T(8,128)} %param.23, s32[]{:T(128)S(6)} %select_n.102, s32[]{:T(128)S(6)} %select_n.104, s32[]{:T(128)S(6)} %select_n.105, ...), kind=kLoop, calls=%fused_computation.101 | loop fusion | flops 99 | bytes 73 | tf_op jit(solution)/shard_map/reduce_or | solution.py:36
  56.7 1.6 %fusion.64 = (s32[1]{0:T(128)}, s32[1]{0:T(128)}, s32[1]{0:T(128)}, s32[1]{0:T(128)}, s32[1]{0:T(128)}, /*index=5*/s32[1]{0:T(128)}, s32[1]{0:T(128)}, s32[1]{0:T(128)}) fusion(s32[32]{0:T(128)} %param.22, s32[]{:T(128)S(6)} %select_n.117, s32[]{:T(128)S(6)} %select_n.116, s32[]{:T(128)S(6)} %select_n.115, s32[]{:T(128)S(6)} %select_n.114, ...), kind=kLoop, calls=%fused_computation.130 | loop fusion | bytes 96 | tf_op jit(solution)/shard_map/jit(dynamic_index_in_dim)/dynamic_slice | solution.py:37
  58.3 0.6 iota_compare_fusion.7
  58.9 1.4 %multiply_reduce_fusion.9 = f32[512]{0:T(512)S(1)} fusion(bf16[512,768]{1,0:T(8,128)(2,1)} %param.21), kind=kLoop, calls=%fused_computation.100 | loop fusion | flops 1179136 | bytes 788480 | tf_op jit(solution)/shard_map/reduce_sum | solution.py:21
  60.2 6.3 %collective-permute-done.4 = bf16[512,768]{1,0:T(8,128)(2,1)} collective-permute-done((bf16[512,768]{1,0:T(8,128)(2,1)S(1)}, bf16[512,768]{1,0:T(8,128)(2,1)}, u32[]{:S(2)}, u32[]{:S(2)}) %collective-permute-start.4) | collective-permute-done | bytes 786464 | tf_op jit(solution)/shard_map/ppermute | solution.py:16
  66.5 0.0 collective-permute-start.6
  67.1 0.0 collective-permute-done.5
  67.1 5.4 %collective-permute-start.7 = (bf16[512,768]{1,0:T(8,128)(2,1)}, bf16[512,768]{1,0:T(8,128)(2,1)}, u32[]{:S(2)}, u32[]{:S(2)}) collective-permute-start(bf16[512,768]{1,0:T(8,128)(2,1)} %collective-permute-done.5), channel_id=1, source_target_pairs={{1,0},{2,1},{3,2},{4,3},{5,4},{6,5},{7,6},{8,7},{9,8},{10,9},{11,1... | collective-permute-start | bytes 2359304 | tf_op jit(solution)/shard_map/ppermute | solution.py:16
  72.5 4.9 %conditional.9 = (f32[512]{0:T(512)S(1)}, f32[512,768]{1,0:T(8,128)S(1)}) conditional(s32[]{:T(128)} %convert_element_type.95, () %tuple.64, (pred[]{:T(512)}, pred[512]{0:T(512)(128)(4,1)S(1)}, bf16[512,768]{1,0:T(8,128)(2,1)}, f32[512]{0:T(512)S(1)}) %tuple.65), branch_computations={%region_10.11_spmd, %region_11.14_spmd} | conditional | flops 808321024 | bytes 8140333 | solution.py:55
  72.5 1.4 %multiply_reduce_fusion = f32[512]{0:T(512)S(1)} fusion(bf16[512,768]{1,0:T(8,128)(2,1)} %get-tuple-element.154), kind=kLoop, calls=%fused_computation | loop fusion | flops 1179136 | bytes 788480 | tf_op jit(solution)/shard_map/cond/branch_1_fun/reduce_sum | solution.py:21
  73.9 0.6 broadcast_and_fusion
  74.5 0.0 copy-start
  74.6 2.3 %fusion.55 = (f32[512]{0:T(512)S(1)}, bf16[512,512]{0,1:T(8,128)(2,1)S(1)}) fusion(f32[512]{0:T(512)S(1)} %add_rsqrt_fusion, f32[512]{0:T(512)S(1)} %get-tuple-element.155, bf16[512,768]{1,0:T(8,128)(2,1)} %get-tuple-element.154, pred[512]{0:T(512)(128)(4,1)S(1)} %broadcast_and_fusion), kind=kOutput, calls=%fused_computation.121 | convolution fusion | flops 404487680 | bytes 1317376 | tf_op jit(solution)/shard_map/cond/branch_1_fun/dot_general | solution.py:42
  76.9 0.6 fusion.5
  77.5 0.6 iota_compare_fusion.6
  78.1 0.6 iota_compare_fusion.5
  78.7 0.6 iota_compare_fusion.4
  79.3 0.6 iota_compare_fusion.3
  79.9 0.7 iota_compare_fusion.2
  80.6 0.6 iota_compare_fusion.1
  81.2 0.6 iota_compare_fusion
  81.8 3.4 %conditional.10 = ((f32[512]{0:T(512)S(1)}, f32[512,768]{1,0:T(8,128)S(1)})) conditional(s32[]{:T(128)} %convert_element_type.94, (f32[512]{0:T(512)S(1)}, f32[512,768]{1,0:T(8,128)S(1)}) %conditional.9, (pred[]{:T(512)}, pred[512]{0:T(512)(128)(4,1)S(1)}, bf16[512,768]{1,0:T(8,128)(2,1)}, bf16[512,768]{1,0:T(8,128)(2,1)S(1)}, f32[512]{0:T(512)S(1)}, ...), branch_computations={%region_14.15_spmd, %region_15.18_spmd} | conditional | flops 808714752 | bytes 7360025 | solution.py:55
  81.8 0.2 multiply_reduce_fusion.1
  82.0 0.6 broadcast_and_fusion.1
  82.7 1.9 %fusion.56 = (f32[512]{0:T(512)S(1)}, bf16[512,512]{0,1:T(8,128)(2,1)S(1)}) fusion(f32[512]{0:T(512)S(1)} %add_rsqrt_fusion.1, f32[512]{0:T(512)S(1)} %get-tuple-element.161, bf16[512,768]{1,0:T(8,128)(2,1)} %get-tuple-element.159, bf16[512,768]{1,0:T(8,128)(2,1)S(1)} %get-tuple-element.160, pred[512]{0:T(512)(128)(4,1)S(1)} %broadcast_and_fusion.1), kind=kOutput, calls=%fused_computation.122 | convolution fusion | flops 404487680 | bytes 2103808 | tf_op jit(solution)/shard_map/cond/branch_1_fun/dot_general | solution.py:42
  84.6 0.6 convolution_add_fusion
  85.3 1.1 copy-done.2
  86.4 3.4 %conditional.13 = ((f32[512]{0:T(512)S(1)}, f32[512,768]{1,0:T(8,128)S(1)})) conditional(s32[]{:T(128)} %convert_element_type.91, (f32[512]{0:T(512)S(1)}, f32[512,768]{1,0:T(8,128)S(1)}) %get-tuple-element.354, (pred[]{:T(512)}, pred[512]{0:T(512)(128)(4,1)S(1)}, bf16[512,768]{1,0:T(8,128)(2,1)}, bf16[512,768]{1,0:T(8,128)(2,1)S(1)}, ...), branch_computations={%region_26.27_spmd, %region_27.30_spmd} | conditional | flops 808714752 | bytes 7360025 | solution.py:55
  86.4 0.2 multiply_reduce_fusion.4
  86.6 0.6 broadcast_and_fusion.4
  87.2 1.9 %fusion.59 = (f32[512]{0:T(512)S(1)}, bf16[512,512]{0,1:T(8,128)(2,1)S(1)}) fusion(f32[512]{0:T(512)S(1)} %add_rsqrt_fusion.4, f32[512]{0:T(512)S(1)} %get-tuple-element.182, bf16[512,768]{1,0:T(8,128)(2,1)} %get-tuple-element.180, bf16[512,768]{1,0:T(8,128)(2,1)S(1)} %get-tuple-element.181, pred[512]{0:T(512)(128)(4,1)S(1)} %broadcast_and_fusion.4), kind=kOutput, calls=%fused_computation.125 | convolution fusion | flops 404487680 | bytes 2103808 | tf_op jit(solution)/shard_map/cond/branch_1_fun/dot_general | solution.py:42
  89.1 0.6 convolution_add_fusion.3
  89.8 6.0 %conditional.15 = ((f32[512]{0:T(512)S(1)}, f32[512,768]{1,0:T(8,128)S(1)})) conditional(s32[]{:T(128)} %convert_element_type.89, (f32[512]{0:T(512)S(1)}, f32[512,768]{1,0:T(8,128)S(1)}) %get-tuple-element.356, (pred[]{:T(512)}, pred[512]{0:T(512)(128)(4,1)S(1)}, bf16[512,768]{1,0:T(8,128)(2,1)}, bf16[512,768]{1,0:T(8,128)(2,1)}, ...), branch_computations={%region_34.35_spmd, %region_35.38_spmd} | conditional | flops 808714752 | bytes 7360025 | solution.py:55
  89.8 1.4 %multiply_reduce_fusion.6 = f32[512]{0:T(512)S(1)} fusion(bf16[512,768]{1,0:T(8,128)(2,1)} %get-tuple-element.195), kind=kLoop, calls=%fused_computation.66 | loop fusion | flops 1179136 | bytes 788480 | tf_op jit(solution)/shard_map/cond/branch_1_fun/reduce_sum | solution.py:21
  91.1 0.6 broadcast_and_fusion.6
  91.8 2.1 %fusion.61 = (f32[512]{0:T(512)S(1)}, bf16[512,512]{0,1:T(8,128)(2,1)S(1)}) fusion(f32[512]{0:T(512)S(1)} %add_rsqrt_fusion.6, f32[512]{0:T(512)S(1)} %get-tuple-element.196, bf16[512,768]{1,0:T(8,128)(2,1)} %get-tuple-element.194, bf16[512,768]{1,0:T(8,128)(2,1)} %get-tuple-element.195, pred[512]{0:T(512)(128)(4,1)S(1)} %broadcast_and_fusion.6), kind=kOutput, calls=%fused_computation.127 | convolution fusion | flops 404487680 | bytes 2103808 | tf_op jit(solution)/shard_map/cond/branch_1_fun/dot_general | solution.py:42
  93.9 1.8 %convolution_add_fusion.5 = f32[512,768]{1,0:T(8,128)S(1)} fusion(f32[512,768]{1,0:T(8,128)S(1)} %get-tuple-element.197, bf16[512,768]{1,0:T(8,128)(2,1)} %get-tuple-element.195, bf16[512,512]{0,1:T(8,128)(2,1)S(1)} %get-tuple-element.285), kind=kOutput, calls=%fused_computation.67 | convolution fusion | flops 403046400 | bytes 4456448 | tf_op jit(solution)/shard_map/cond/branch_1_fun/dot_general | solution.py:50
  95.7 0.0 collective-permute-done.6
  95.7 0.0 copy-start.5
  95.8 6.1 %conditional.16 = ((f32[512]{0:T(512)S(1)}, f32[512,768]{1,0:T(8,128)S(1)})) conditional(s32[]{:T(128)} %convert_element_type.88, (f32[512]{0:T(512)S(1)}, f32[512,768]{1,0:T(8,128)S(1)}) %get-tuple-element.357, (pred[]{:T(512)}, pred[512]{0:T(512)(128)(4,1)S(1)}, bf16[512,768]{1,0:T(8,128)(2,1)}, bf16[512,768]{1,0:T(8,128)(2,1)}, ...), branch_computations={%region_38.39_spmd, %region_39.42_spmd} | conditional | flops 808714752 | bytes 7360025 | solution.py:55
  96.0 1.4 %multiply_reduce_fusion.7 = f32[512]{0:T(512)S(1)} fusion(bf16[512,768]{1,0:T(8,128)(2,1)} %get-tuple-element.202), kind=kLoop, calls=%fused_computation.77 | loop fusion | flops 1179136 | bytes 788480 | tf_op jit(solution)/shard_map/cond/branch_1_fun/reduce_sum | solution.py:21
  97.3 0.6 broadcast_and_fusion.7
  97.9 2.2 %fusion.62 = (f32[512]{0:T(512)S(1)}, bf16[512,512]{0,1:T(8,128)(2,1)S(1)}) fusion(f32[512]{0:T(512)S(1)} %add_rsqrt_fusion.7, f32[512]{0:T(512)S(1)} %get-tuple-element.203, bf16[512,768]{1,0:T(8,128)(2,1)} %get-tuple-element.201, bf16[512,768]{1,0:T(8,128)(2,1)} %get-tuple-element.202, pred[512]{0:T(512)(128)(4,1)S(1)} %broadcast_and_fusion.7), kind=kOutput, calls=%fused_computation.128 | convolution fusion | flops 404487680 | bytes 2103808 | tf_op jit(solution)/shard_map/cond/branch_1_fun/dot_general | solution.py:42
  100.1 1.8 %convolution_add_fusion.6 = f32[512,768]{1,0:T(8,128)S(1)} fusion(f32[512,768]{1,0:T(8,128)S(1)} %get-tuple-element.204, bf16[512,768]{1,0:T(8,128)(2,1)} %get-tuple-element.202, bf16[512,512]{0,1:T(8,128)(2,1)S(1)} %get-tuple-element.287), kind=kOutput, calls=%fused_computation.78 | convolution fusion | flops 403046400 | bytes 4456448 | tf_op jit(solution)/shard_map/cond/branch_1_fun/dot_general | solution.py:50
  101.9 0.0 collective-permute-done.7
  101.9 7.2 %conditional.17 = ((f32[512]{0:T(512)S(1)}, f32[512,768]{1,0:T(8,128)S(1)})) conditional(s32[]{:T(128)} %convert_element_type.87, (f32[512]{0:T(512)S(1)}, f32[512,768]{1,0:T(8,128)S(1)}) %get-tuple-element.358, (pred[]{:T(512)}, s32[512]{0:T(512)S(1)}, bf16[512,768]{1,0:T(8,128)(2,1)}, bf16[512,768]{1,0:T(8,128)(2,1)}, f32[512]{0:T(512)S(1)}, ...), branch_computations={%region_42.43_spmd, %region_43.46_spmd} | conditional | flops 808715264 | bytes 7361611 | solution.py:55
  101.9 1.4 %multiply_reduce_fusion.8 = f32[512]{0:T(512)S(1)} fusion(bf16[512,768]{1,0:T(8,128)(2,1)} %get-tuple-element.209), kind=kLoop, calls=%fused_computation.88 | loop fusion | flops 1179136 | bytes 788480 | tf_op jit(solution)/shard_map/cond/branch_1_fun/reduce_sum | solution.py:21
  103.3 0.6 dynamic_slice.43
  103.9 1.3 %compare_and_fusion = pred[512]{0:T(512)(128)(4,1)S(1)} fusion(s32[512]{0:T(512)S(1)} %get-tuple-element.250, s32[]{:T(128)} %bitcast, pred[]{:T(512)} %get-tuple-element.207), kind=kLoop, calls=%fused_computation.98 | loop fusion | flops 1024 | bytes 2565 | tf_op jit(solution)/shard_map/cond/branch_1_fun/and | solution.py:46
  105.2 2.1 %fusion.63 = (f32[512]{0:T(512)S(1)}, bf16[512,512]{0,1:T(8,128)(2,1)S(1)}) fusion(f32[512]{0:T(512)S(1)} %add_rsqrt_fusion.8, f32[512]{0:T(512)S(1)} %get-tuple-element.210, bf16[512,768]{1,0:T(8,128)(2,1)} %get-tuple-element.208, bf16[512,768]{1,0:T(8,128)(2,1)} %get-tuple-element.209, pred[512]{0:T(512)(128)(4,1)S(1)} %compare_and_fusion), kind=kOutput, calls=%fused_computation.129 | convolution fusion | flops 404487680 | bytes 2103808 | tf_op jit(solution)/shard_map/cond/branch_1_fun/dot_general | solution.py:42
  107.3 1.8 %convolution_add_fusion.7 = f32[512,768]{1,0:T(8,128)S(1)} fusion(f32[512,768]{1,0:T(8,128)S(1)} %get-tuple-element.211, bf16[512,768]{1,0:T(8,128)(2,1)} %get-tuple-element.209, bf16[512,512]{0,1:T(8,128)(2,1)S(1)} %get-tuple-element.289), kind=kOutput, calls=%fused_computation.89 | convolution fusion | flops 403046400 | bytes 4456448 | tf_op jit(solution)/shard_map/cond/branch_1_fun/dot_general | solution.py:50
  109.1 1.1 %broadcast_select_fusion = f32[512]{0:T(512)} fusion(f32[512]{0:T(512)S(1)} %get-tuple-element.248, s32[]{:T(128)} %bitcast.1), kind=kLoop, calls=%fused_computation.119 | loop fusion | flops 1024 | bytes 4100 | tf_op jit(solution)/shard_map/jit(_where)/select_n | solution.py:73
  110.2 1.1 select_convert_fusion
  (22 shorter events, 0.1 us)
Async XLA Ops:
  0.6 22.1 %collective-permute-start = (bf16[512,768]{1,0:T(8,128)(2,1)}, bf16[512,768]{1,0:T(8,128)(2,1)S(1)}, u32[]{:S(2)}, u32[]{:S(2)}) collective-permute-start(bf16[512,768]{1,0:T(8,128)(2,1)} %param.21), channel_id=1, source_target_pairs={{31,0},{0,1},{1,2},{2,3},{3,4},{4,5},{5,6},{6,7},{7,8},{8,9},{9,10... | collective-permute-start | bytes 2359304 | tf_op jit(solution)/shard_map/ppermute | solution.py:16
  1.1 21.6 %collective-permute-start.1 = (bf16[512,768]{1,0:T(8,128)(2,1)}, bf16[512,768]{1,0:T(8,128)(2,1)S(1)}, u32[]{:S(2)}, u32[]{:S(2)}) collective-permute-start(bf16[512,768]{1,0:T(8,128)(2,1)} %param.21), channel_id=1, source_target_pairs={{1,0},{2,1},{3,2},{4,3},{5,4},{6,5},{7,6},{8,7},{9,8},{10,9},{11,1... | collective-permute-start | bytes 2359304 | tf_op jit(solution)/shard_map/ppermute | solution.py:16
  22.7 22.1 %collective-permute-start.2 = (bf16[512,768]{1,0:T(8,128)(2,1)S(1)}, bf16[512,768]{1,0:T(8,128)(2,1)S(1)}, u32[]{:S(2)}, u32[]{:S(2)}) collective-permute-start(bf16[512,768]{1,0:T(8,128)(2,1)S(1)} %collective-permute-done), channel_id=1, source_target_pairs={{31,0},{0,1},{1,2},{2,3},{3,4},{4,5},{5,6},{6,7},{7,8},{8,9},{9,10... | collective-permute-start | bytes 2359304 | tf_op jit(solution)/shard_map/ppermute | solution.py:16
  22.7 22.1 %copy-start.3 = (bf16[512,768]{1,0:T(8,128)(2,1)}, bf16[512,768]{1,0:T(8,128)(2,1)S(1)}, u32[]{:S(2)}) copy-start(bf16[512,768]{1,0:T(8,128)(2,1)S(1)} %collective-permute-done.1) | copy-start | bytes 2359300
  22.7 22.1 %collective-permute-start.3 = (bf16[512,768]{1,0:T(8,128)(2,1)S(1)}, bf16[512,768]{1,0:T(8,128)(2,1)S(1)}, u32[]{:S(2)}, u32[]{:S(2)}) collective-permute-start(bf16[512,768]{1,0:T(8,128)(2,1)S(1)} %collective-permute-done.1), channel_id=1, source_target_pairs={{1,0},{2,1},{3,2},{4,3},{5,4},{6,5},{7,6},{8,7},{9,8},{10,9},{11,1... | collective-permute-start | bytes 2359304 | tf_op jit(solution)/shard_map/ppermute | solution.py:16
  44.8 27.8 %copy-start.1 = (bf16[512,768]{1,0:T(8,128)(2,1)}, bf16[512,768]{1,0:T(8,128)(2,1)S(1)}, u32[]{:S(2)}) copy-start(bf16[512,768]{1,0:T(8,128)(2,1)S(1)} %collective-permute-done.2) | copy-start | bytes 2359300
  44.8 21.7 %collective-permute-start.4 = (bf16[512,768]{1,0:T(8,128)(2,1)S(1)}, bf16[512,768]{1,0:T(8,128)(2,1)}, u32[]{:S(2)}, u32[]{:S(2)}) collective-permute-start(bf16[512,768]{1,0:T(8,128)(2,1)S(1)} %collective-permute-done.2), channel_id=1, source_target_pairs={{31,0},{0,1},{1,2},{2,3},{3,4},{4,5},{5,6},{6,7},{7,8},{8,9},{9,10... | collective-permute-start | bytes 2359304 | tf_op jit(solution)/shard_map/ppermute | solution.py:16
  44.8 22.4 %collective-permute-start.5 = (bf16[512,768]{1,0:T(8,128)(2,1)S(1)}, bf16[512,768]{1,0:T(8,128)(2,1)}, u32[]{:S(2)}, u32[]{:S(2)}) collective-permute-start(bf16[512,768]{1,0:T(8,128)(2,1)S(1)} %collective-permute-done.3), channel_id=1, source_target_pairs={{1,0},{2,1},{3,2},{4,3},{5,4},{6,5},{7,6},{8,7},{9,8},{10,9},{11,1... | collective-permute-start | bytes 2359304 | tf_op jit(solution)/shard_map/ppermute | solution.py:16
  66.5 29.2 %collective-permute-start.6 = (bf16[512,768]{1,0:T(8,128)(2,1)}, bf16[512,768]{1,0:T(8,128)(2,1)}, u32[]{:S(2)}, u32[]{:S(2)}) collective-permute-start(bf16[512,768]{1,0:T(8,128)(2,1)} %collective-permute-done.4), channel_id=1, source_target_pairs={{31,0},{0,1},{1,2},{2,3},{3,4},{4,5},{5,6},{6,7},{7,8},{8,9},{9,10... | collective-permute-start | bytes 2359304 | tf_op jit(solution)/shard_map/ppermute | solution.py:16
  67.1 34.7 %collective-permute-start.7 = (bf16[512,768]{1,0:T(8,128)(2,1)}, bf16[512,768]{1,0:T(8,128)(2,1)}, u32[]{:S(2)}, u32[]{:S(2)}) collective-permute-start(bf16[512,768]{1,0:T(8,128)(2,1)} %collective-permute-done.5), channel_id=1, source_target_pairs={{1,0},{2,1},{3,2},{4,3},{5,4},{6,5},{7,6},{8,7},{9,8},{10,9},{11,1... | collective-permute-start | bytes 2359304 | tf_op jit(solution)/shard_map/ppermute | solution.py:16
  74.5 2.3 %copy-start = (bf16[512,768]{1,0:T(8,128)(2,1)S(1)}, bf16[512,768]{1,0:T(8,128)(2,1)}, u32[]{:S(2)}) copy-start(bf16[512,768]{1,0:T(8,128)(2,1)} %get-tuple-element.154) | copy-start | bytes 2359300 | tf_op jit(solution)/shard_map/cond
  85.2 1.1 %copy-start.2 = (bf16[512,768]{1,0:T(8,128)(2,1)S(1)}, bf16[512,768]{1,0:T(8,128)(2,1)}, u32[]{:S(2)}) copy-start(bf16[512,768]{1,0:T(8,128)(2,1)} %copy-done.1) | copy-start | bytes 2359300
  95.7 6.2 %copy-start.5 = (s32[32]{0:T(128)S(1)}, s32[32]{0:T(128)}, u32[]{:S(2)}) copy-start(s32[32]{0:T(128)} %param.22) | copy-start | bytes 388
where the time goes:
time: 111 us
  waiting for transfers between devices  38.6 us (35%)
  starting transfers between devices  22.6 us (20%)
  other arithmetic  20.4 us (18%)
  matrix products  19.7 us (18%)
  between operations  6.42 us (6%)
  local copies, waits for them, and re-layouts  3.35 us (3%)
    ppermute x8, waiting for transfers between devices, passed_along(): return lax.ppermute(block, axis, route)  38.6 us
    ppermute x8, starting transfers between devices, passed_along(): return lax.ppermute(block, axis, route)  22.6 us
    dot_general x6, matrix products, tile_work(): lax.dot_general(embeddings, arrived, (((1,), (1,)), ((), ())), preferred_...  12.6 us
    reduce_sum x7, other arithmetic, reciprocal_norms(): return lax.rsqrt(jnp.sum(values * values, axis=1) + epsilon)  7.26 us
    dot_general x6, matrix products, tile_work(): jnp.dot(coupling_factor.astype(jnp.bfloat16), arrived, preferred_element_...  7.12 us
    and x6, other arithmetic, tile_work(): eligible_couplings = column_valid[None, :] & is_listed  4.35 us
    lt x7, other arithmetic, add_tile(): column_valid = slot_index < column_count  4.28 us
    dynamic_slice x2, local copies, waits for them, and re-layouts, add_tile(): column_count = lax.dynamic_index_in_dim(counts, source, 0, keepdims=False)  2.22 us
  transfers between devices with their start and end apart: 8, of which 3 were waited for; matrix products, arithmetic and copies ran while one was open for 30% of the time, Pallas kernels for 0%

commit v1 on v0

v1 whole, which is shorter than its diff:
```python
import functools
import math

import jax
import jax.numpy as jnp
from jax import lax
from jax.experimental import pallas as pl
from jax.experimental.pallas import tpu as pltpu
from jax.sharding import PartitionSpec as P

MESH = pl.DeviceIdType.MESH

smoothing_scale = 4.0
epsilon = 1e-06
LOG2E = math.log2(math.e)
BLOCKED = -1e30

P2, P1, N1, N2 = 0, 1, 2, 3
OFFSET = (-2, -1, 1, 2)
SIB = 8
PIECES = 4
TILE = 256


def kernel(row_total, col_total, e_ref, counts_ref, pairs_ref, dens_ref, out_ref,
           held, acc, tot, scale, send_own, send_link, send_sib, recv):
    rows, width = e_ref.shape
    piece = rows // PIECES
    tiles = rows // TILE
    pieces_per_tile = PIECES // tiles
    chips = col_total // 2
    chip_total = row_total * chips
    block_total = row_total * col_total
    row = lax.axis_index("row")
    col = lax.axis_index("col")
    z = col // 2
    core = col % 2
    chip = row * chips + z
    me = row * col_total + col
    lines = chips == 4 and row_total >= 3

    def device(where, lane):
        where = lax.rem(where + 2 * chip_total, chip_total)
        return {"row": where // chips, "col": lax.rem(where, chips) * 2 + lane}

    sibling = device(chip, 1 - core)
    above = device(chip + 1, core)
    below = device(chip - 1, core)
    next_line = device(chip + chips, core)
    last_line = device(chip - chips, core)

    def when(condition, action):
        if condition is True:
            action()
        elif condition is not False:
            pl.when(condition)(action)

    if lines:
        has_below, has_above = z > 0, z < 3
        middle = (z == 1) | (z == 2)
        low, high = z < 2, z >= 2
        ends = (z == 0) | (z == 3)
    else:
        has_below = has_above = middle = True

    barrier = pltpu.get_barrier_semaphore()

    def greet(who):
        pl.semaphore_signal(barrier, inc=1, device_id=who, device_id_type=MESH)

    greet(sibling)
    when(has_above, lambda: greet(above))
    when(has_below, lambda: greet(below))
    if lines:
        greet(next_line)
        greet(last_line)
        when(middle, lambda: pl.semaphore_wait(barrier, 5))
        when(ends, lambda: pl.semaphore_wait(barrier, 4))
    else:
        pl.semaphore_wait(barrier, 3)

    def part(k):
        return pl.ds(pl.multiple_of(k * piece, piece), piece)

    def copy(src, slot, k, send, who):
        return pltpu.make_async_remote_copy(
            src_ref=src.at[part(k)], dst_ref=held.at[slot, part(k)],
            send_sem=send.at[k], recv_sem=recv.at[slot, k],
            device_id=who, device_id_type=MESH)

    mine = core * 4
    other = (1 - core) * 4

    def own_up(k):
        return copy(e_ref, mine + P1, k, send_own.at[0], above)

    def own_down(k):
        return copy(e_ref, mine + N1, k, send_own.at[1], below)

    def own_sib(k):
        return copy(e_ref, SIB, k, send_own.at[2], sibling)

    def relay(slot, to_slot, k, who):
        return copy(held.at[mine + slot], mine + to_slot, k, send_link.at[slot], who)

    def share(slot, k):
        return copy(held.at[mine + slot], mine + slot, k, send_sib.at[slot], sibling)

    def await_piece(slot, k):
        copy(e_ref, slot, k, send_own.at[0], sibling).wait_recv()

    def each(n, action):
        lax.fori_loop(0, n, lambda k, c: (action(k), c)[1], 0)

    def start_own(k):
        when(has_below, lambda: own_down(k).start())
        when(has_above, lambda: own_up(k).start())
        own_sib(k).start()

    each(PIECES, start_own)

    def limit(block):
        listed = jnp.int32(0)
        for j in range(pairs_ref.shape[1]):
            listed = listed | jnp.where(pairs_ref[me, j] == block, 1, 0)
        return counts_ref[block] * listed

    def inverse(x):
        x = x.astype(jnp.float32)
        return lax.rsqrt(jnp.sum(x * x, axis=1, keepdims=True) + epsilon)

    def one_tile(x, block, t):
        size = x.shape[0]
        column = jnp.transpose(jnp.broadcast_to(inverse(x), (size, 128)))[0:1, :]
        slot_index = lax.broadcasted_iota(jnp.int32, (1, size), 1) + t * TILE
        shift = jnp.where(slot_index < limit(block), -smoothing_scale * LOG2E, BLOCKED)
        products = lax.dot_general(
            e_ref[...], x, (((1,), (1,)), ((), ())), preferred_element_type=jnp.float32)
        weight = jnp.exp2(products * scale[...] * column + shift)
        folded = weight[:, :128]
        for j in range(1, size // 128):
            folded = folded + weight[:, j * 128:(j + 1) * 128]
        tot[...] += folded
        acc[...] += jnp.dot(weight.astype(jnp.bfloat16), x, preferred_element_type=jnp.float32)

    def tile_rows(t):
        return pl.ds(pl.multiple_of(t * TILE, TILE), TILE)

    def held_tile(slot, block, t):
        one_tile(held[slot, tile_rows(t), :], block, t)

    def owner(slot, lane):
        return lax.rem(chip * 2 + 2 * offset_of(slot) + lane + block_total, block_total)

    def offset_of(slot):
        if isinstance(slot, int):
            return OFFSET[slot]
        return slot - 2 + slot // 2

    def own_lane_tile(slot, t):
        held_tile(mine + slot, owner(slot, core), t)

    def other_lane_tile(slot, t):
        for j in range(pieces_per_tile):
            await_piece(other + slot, t * pieces_per_tile + j)
        held_tile(other + slot, owner(slot, 1 - core), t)

    def both_tiles(slot, t):
        def go(lane, c):
            here = lax.rem(core + lane, 2)

            @pl.when(lane == 1)
            def _():
                for j in range(pieces_per_tile):
                    await_piece(here * 4 + slot, t * pieces_per_tile + j)

            held_tile(here * 4 + slot, owner(slot, here), t)
            return c

        lax.fori_loop(0, 2, go, 0)

    scale[...] = jnp.broadcast_to(
        inverse(e_ref[...]) * (smoothing_scale * LOG2E), scale.shape)
    acc[...] = jnp.zeros_like(acc)
    tot[...] = jnp.zeros_like(tot)

    each(tiles, lambda t: one_tile(e_ref[tile_rows(t), :], me, t))

    def sib_tile(t):
        for j in range(pieces_per_tile):
            await_piece(SIB, t * pieces_per_tile + j)
        held_tile(SIB, me + 1 - 2 * core, t)

    each(tiles, sib_tile)

    def near(k):
        def from_above():
            await_piece(mine + N1, k)
            when(middle, lambda: relay(N1, N2, k, below).start())
            share(N1, k).start()

        def from_below():
            await_piece(mine + P1, k)
            when(middle, lambda: relay(P1, P2, k, above).start())
            share(P1, k).start()

        when(has_above, from_above)
        when(has_below, from_below)

    each(PIECES, near)

    per = PIECES // tiles

    def take_far_above(k):
        await_piece(mine + N2, k)
        if lines:
            when(low, lambda: relay(N2, P2, k, next_line).start())
            when(z == 2, lambda: relay(N2, N1, k, above).start())
        when(core == 0, lambda: share(N2, k).start())

    def take_far_below(k):
        await_piece(mine + P2, k)
        if lines:
            when(high, lambda: relay(P2, N2, k, last_line).start())
            when(z == 1, lambda: relay(P2, P1, k, below).start())
        when(core == 1, lambda: share(P2, k).start())

    def far(k):
        if lines:
            when(high, lambda: take_far_below(k))
            take_far_above(k)
            when(low, lambda: take_far_below(k))
        else:
            take_far_above(k)
            take_far_below(k)

    def spread(k, slots, job):
        steps = PIECES // 2
        t_per = tiles // steps if tiles >= steps else 1
        which = k // steps
        base = (k % steps) * t_per
        for j in range(t_per):
            job(slots(which), base + j)

    def second(k):
        far(k)
        slot = N1 - k // (PIECES // 2)
        t = k % (PIECES // 2)
        if lines:
            skip = ((z == 0) & (slot == P1)) | ((z == 3) & (slot == N1))
            when(jnp.logical_not(skip), lambda: both_tiles(slot, t))
        else:
            both_tiles(slot, t)

    each(PIECES, second)

    if lines:
        last = jnp.where(z == 0, P1, N1)

    def third(k):
        if lines:
            def take():
                await_piece(mine + last, k)
                share_last(k).start()

            when(ends, take)
        slot = N2 * (k // (PIECES // 2))
        t = k % (PIECES // 2)
        own_lane_tile(slot, t)

    def share_last(k):
        return copy(held.at[mine + last], mine + last, k, send_sib.at[last], sibling)

    def far_other(t):
        slot = N2 * core
        other_lane_tile(slot, t)

    each(tiles, far_other) if not lines else None
    if lines:
        def third_all(k):
            third(k)
            when((k % 2) == 0, lambda: far_other(k // 2))
            when(ends & (k == PIECES - 1), lambda: both_tiles(last, 0))

        each(PIECES, third_all)
        when(ends, lambda: both_tiles(last, tiles - 1))
    else:
        each(PIECES, third)

    total = jnp.sum(tot[...], axis=1, keepdims=True)
    count = counts_ref[me]
    valid = lax.broadcasted_iota(jnp.int32, (rows, 1), 0) < count
    out_ref[...] = jnp.where(valid, acc[...] / total, 0.0).astype(out_ref.dtype)
    across = jnp.transpose(jnp.broadcast_to(total, (rows, 128)))[0:1, :]
    dens_ref[...] = jnp.where(
        lax.broadcasted_iota(jnp.int32, (1, rows), 1) < count, across, 0.0)

    def drain(k):
        when(has_below, lambda: own_down(k).wait_send())
        when(has_above, lambda: own_up(k).wait_send())
        own_sib(k).wait_send()
        when(middle, lambda: relay(N1, N2, k, below).wait_send())
        when(middle, lambda: relay(P1, P2, k, above).wait_send())
        share(N1, k).wait_send()
        share(P1, k).wait_send()
        when(core == 0, lambda: share(N2, k).wait_send())
        when(core == 1, lambda: share(P2, k).wait_send())
        if lines:
            when(z < 3, lambda: relay(N2, P2, k, next_line).wait_send())
            when(z > 0, lambda: relay(P2, N2, k, last_line).wait_send())

    each(PIECES, drain)


def solution(mesh):
    row_total, col_total = mesh.shape["row"], mesh.shape["col"]

    def body(embeddings, counts, pairs):
        rows, width = embeddings.shape
        density, neighbour = pl.pallas_call(
            functools.partial(kernel, row_total, col_total),
            out_shape=(jax.ShapeDtypeStruct((1, rows), jnp.float32),
                       jax.ShapeDtypeStruct((rows, width), jnp.bfloat16)),
            in_specs=[pl.BlockSpec(memory_space=pltpu.VMEM),
                      pl.BlockSpec(memory_space=pltpu.SMEM),
                      pl.BlockSpec(memory_space=pltpu.SMEM)],
            out_specs=(pl.BlockSpec(memory_space=pltpu.VMEM),
                       pl.BlockSpec(memory_space=pltpu.VMEM)),
            scratch_shapes=[
                pltpu.VMEM((9, rows, width), jnp.bfloat16),
                pltpu.VMEM((rows, width), jnp.float32),
                pltpu.VMEM((rows, 128), jnp.float32),
                pltpu.VMEM((rows, TILE), jnp.float32),
                pltpu.SemaphoreType.DMA((3, PIECES)),
                pltpu.SemaphoreType.DMA((4, PIECES)),
                pltpu.SemaphoreType.DMA((4, PIECES)),
                pltpu.SemaphoreType.DMA((9, PIECES)),
            ],
            compiler_params=pltpu.CompilerParams(
                collective_id=0, has_side_effects=True, vmem_limit_bytes=48 * 1024 * 1024),
        )(embeddings, counts, pairs)
        return density.reshape(rows), neighbour

    in_specs = (P(("row", "col"), None), P(), P())
    out_specs = (P(("row", "col")), P(("row", "col"), None))
    return jax.shard_map(body, mesh=mesh, in_specs=in_specs, out_specs=out_specs, check_vma=False)
```

time: 111 us -> 70 us (0.63)
  Pallas kernels: 0 us -> 65.8 us
  waiting for transfers between devices: 38.6 us -> 0 us
  starting transfers between devices: 22.6 us -> 0 us
  other arithmetic: 20.4 us -> 0 us
  matrix products: 19.7 us -> 0 us
  between operations: 6.42 us -> 0.65 us
    pallas_call x0 -> x1, Pallas kernels: none -> 65.8 us  [body(): pl.pallas_call(functools.partial(kernel, row_total, col_total), out_shape...]
    ppermute x8 -> x0, waiting for transfers between devices: 38.6 us -> none  [passed_along(): return lax.ppermute(block, axis, route)]
    ppermute x8 -> x0, starting transfers between devices: 22.6 us -> none  [passed_along(): return lax.ppermute(block, axis, route)]
    dot_general x12 -> x0, matrix products: 19.7 us -> none  [the longest x6 12.6 us: tile_work(): lax.dot_general(embeddings, arrived, (((1,), (1,)), ((), ())), preferred_...]
    reduce_sum x7 -> x0, other arithmetic: 7.26 us -> none  [reciprocal_norms(): return lax.rsqrt(jnp.sum(values * values, axis=1) + epsilon)]
    lt x8 -> x0, other arithmetic: 4.83 us -> none  [the longest x7 4.28 us: add_tile(): column_valid = slot_index < column_count]
    and x6 -> x0, other arithmetic: 4.35 us -> none  [tile_work(): eligible_couplings = column_valid[None, :] & is_listed]
    unnamed x8 -> x7, local copies, waits for them, and re-layouts: 1.12 us -> 3.37 us
  transfers between devices with their start and end apart: 8 -> 0, of which waited for: 3 -> 0; matrix products, arithmetic and copies ran while one was open for 30% -> 0% of each run, Pallas kernels for 0% -> 0%
where the time goes in v1:
time: 70 us; the launch traced here: 69.8 us
  Pallas kernels  65.8 us (94%)
  local copies, waits for them, and re-layouts  3.37 us (5%)
    pallas_call x1, Pallas kernels, body(): pl.pallas_call(functools.partial(kernel, row_total, col_total), out_shape...  65.8 us
    unnamed x7, local copies, waits for them, and re-layouts  3.37 us

profile of v1, /device:TPU:0, one launch (start us, length us, event | category | flops | bytes accessed | tf_op | source)
XLA Modules:
  0.0 69.8 jit_solution(14914212792395869260)
XLA Ops:
  0.6 0.0 copy-start.1
  0.6 0.8 %copy.5.pairs_ref = s32[32,6]{1,0:T(8,128)S(1)} copy(s32[32,6]{0,1:T(8,128)} %param.5) | data formatting | bytes 1536 | tf_op args[2]
  1.4 0.0 copy-done.1
  1.4 0.0 copy-start
  1.4 1.1 %copy-done = bf16[512,768]{1,0:T(8,128)(2,1)S(1)} copy-done((bf16[512,768]{1,0:T(8,128)(2,1)S(1)}, bf16[512,768]{1,0:T(8,128)(2,1)}, u32[]{:S(2)}) %copy-start) | copy-done | bytes 786456
  2.6 65.8 %shard_map.50 = (f32[1,512]{1,0:T(1,128)S(1)}, bf16[512,768]{1,0:T(8,128)(2,1)S(1)}) custom-call(bf16[512,768]{1,0:T(8,128)(2,1)S(1)} %copy-done, s32[32]{0:T(128)S(1)} %copy-done.1, s32[32,6]{1,0:T(8,128)S(1)} %copy.5.pairs_ref), custom_call_target="tpu_custom_call" | custom-call | tf_op jit(solution)/shard_map/pallas_call | solution.py:320
  68.4 0.6 copy.8
  69.0 0.9 %copy.9 = bf16[512,768]{1,0:T(8,128)(2,1)} copy(bf16[512,768]{1,0:T(8,128)(2,1)S(1)} %get-tuple-element.9) | data formatting | bytes 1572864
Async XLA Ops:
  0.6 0.8 %copy-start.1 = (s32[32]{0:T(128)S(1)}, s32[32]{0:T(128)}, u32[]{:S(2)}) copy-start(s32[32]{0:T(128)} %counts_ref.1) | copy-start | bytes 388
  1.4 1.1 %copy-start = (bf16[512,768]{1,0:T(8,128)(2,1)S(1)}, bf16[512,768]{1,0:T(8,128)(2,1)}, u32[]{:S(2)}) copy-start(bf16[512,768]{1,0:T(8,128)(2,1)} %e_ref.1) | copy-start | bytes 2359300

commit v2 on v1

--- a/solution.py
+++ b/solution.py
@@ -19,15 +19,12 @@
 OFFSET = (-2, -1, 1, 2)
 SIB = 8
 PIECES = 4
-TILE = 256
-
-
-def kernel(row_total, col_total, e_ref, counts_ref, pairs_ref, dens_ref, out_ref,
-           held, acc, tot, scale, send_own, send_link, send_sib, recv):
+
+
+def kernel(row_total, col_total, e_hbm, counts_ref, pairs_hbm, dens_ref, out_ref,
+           e_ref, pairs_ref, held, acc, tot, scale, local, send_own, send_link, send_sib, recv):
     rows, width = e_ref.shape
     piece = rows // PIECES
-    tiles = rows // TILE
-    pieces_per_tile = PIECES // tiles
     chips = col_total // 2
     chip_total = row_total * chips
     block_total = row_total * col_total
@@ -63,6 +60,10 @@
     else:
         has_below = has_above = middle = True
 
+    load_own = pltpu.make_async_copy(e_hbm, e_ref, local.at[0])
+    load_pairs = pltpu.make_async_copy(pairs_hbm, pairs_ref, local.at[1])
+    load_own.start()
+    load_pairs.start()
     barrier = pltpu.get_barrier_semaphore()
 
     def greet(who):
@@ -92,13 +93,13 @@
     other = (1 - core) * 4
 
     def own_up(k):
-        return copy(e_ref, mine + P1, k, send_own.at[0], above)
+        return copy(e_hbm, mine + P1, k, send_own.at[0], above)
 
     def own_down(k):
-        return copy(e_ref, mine + N1, k, send_own.at[1], below)
+        return copy(e_hbm, mine + N1, k, send_own.at[1], below)
 
     def own_sib(k):
-        return copy(e_ref, SIB, k, send_own.at[2], sibling)
+        return copy(e_hbm, SIB, k, send_own.at[2], sibling)
 
     def relay(slot, to_slot, k, who):
         return copy(held.at[mine + slot], mine + to_slot, k, send_link.at[slot], who)
@@ -107,7 +108,7 @@
         return copy(held.at[mine + slot], mine + slot, k, send_sib.at[slot], sibling)
 
     def await_piece(slot, k):
-        copy(e_ref, slot, k, send_own.at[0], sibling).wait_recv()
+        copy(e_hbm, slot, k, send_own.at[0], sibling).wait_recv()
 
     def each(n, action):
         lax.fori_loop(0, n, lambda k, c: (action(k), c)[1], 0)
@@ -118,6 +119,8 @@
         own_sib(k).start()
 
     each(PIECES, start_own)
+    load_own.wait()
+    load_pairs.wait()
 
     def limit(block):
         listed = jnp.int32(0)
@@ -129,11 +132,14 @@
         x = x.astype(jnp.float32)
         return lax.rsqrt(jnp.sum(x * x, axis=1, keepdims=True) + epsilon)
 
-    def one_tile(x, block, t):
+    def one_tile(x, bounds, first):
         size = x.shape[0]
         column = jnp.transpose(jnp.broadcast_to(inverse(x), (size, 128)))[0:1, :]
-        slot_index = lax.broadcasted_iota(jnp.int32, (1, size), 1) + t * TILE
-        shift = jnp.where(slot_index < limit(block), -smoothing_scale * LOG2E, BLOCKED)
+        span = size // len(bounds)
+        slot_index = lax.broadcasted_iota(jnp.int32, (1, span), 1) + first
+        valid = [slot_index < bound for bound in bounds]
+        shift = jnp.concatenate(
+            [jnp.where(v, -smoothing_scale * LOG2E, BLOCKED) for v in valid], axis=1)
         products = lax.dot_general(
             e_ref[...], x, (((1,), (1,)), ((), ())), preferred_element_type=jnp.float32)
         weight = jnp.exp2(products * scale[...] * column + shift)
@@ -143,11 +149,8 @@
         tot[...] += folded
         acc[...] += jnp.dot(weight.astype(jnp.bfloat16), x, preferred_element_type=jnp.float32)
 
-    def tile_rows(t):
-        return pl.ds(pl.multiple_of(t * TILE, TILE), TILE)
-
-    def held_tile(slot, block, t):
-        one_tile(held[slot, tile_rows(t), :], block, t)
+    def block_tile(slot, block):
+        one_tile(held[slot], [limit(block)], 0)
 
     def owner(slot, lane):
         return lax.rem(chip * 2 + 2 * offset_of(slot) + lane + block_total, block_total)
@@ -157,41 +160,22 @@
             return OFFSET[slot]
         return slot - 2 + slot // 2
 
-    def own_lane_tile(slot, t):
-        held_tile(mine + slot, owner(slot, core), t)
-
-    def other_lane_tile(slot, t):
-        for j in range(pieces_per_tile):
-            await_piece(other + slot, t * pieces_per_tile + j)
-        held_tile(other + slot, owner(slot, 1 - core), t)
-
-    def both_tiles(slot, t):
-        def go(lane, c):
-            here = lax.rem(core + lane, 2)
-
-            @pl.when(lane == 1)
-            def _():
-                for j in range(pieces_per_tile):
-                    await_piece(here * 4 + slot, t * pieces_per_tile + j)
-
-            held_tile(here * 4 + slot, owner(slot, here), t)
-            return c
-
-        lax.fori_loop(0, 2, go, 0)
+    def await_block(slot):
+        each(PIECES, lambda k: await_piece(slot, k))
+
+    def lane_tile(slot, shared):
+        lane = lax.rem(core + shared, 2)
+        pl.when(shared == 1)(lambda: await_block(lane * 4 + slot))
+        block_tile(lane * 4 + slot, owner(slot, lane))
 
     scale[...] = jnp.broadcast_to(
         inverse(e_ref[...]) * (smoothing_scale * LOG2E), scale.shape)
     acc[...] = jnp.zeros_like(acc)
     tot[...] = jnp.zeros_like(tot)
 
-    each(tiles, lambda t: one_tile(e_ref[tile_rows(t), :], me, t))
-
-    def sib_tile(t):
-        for j in range(pieces_per_tile):
-            await_piece(SIB, t * pieces_per_tile + j)
-        held_tile(SIB, me + 1 - 2 * core, t)
-
-    each(tiles, sib_tile)
+    one_tile(e_ref[...], [limit(me)], 0)
+    await_block(SIB)
+    block_tile(SIB, me + 1 - 2 * core)
 
     def near(k):
         def from_above():
@@ -209,7 +193,6 @@
 
     each(PIECES, near)
 
-    per = PIECES // tiles
 
     def take_far_above(k):
         await_piece(mine + N2, k)
@@ -234,63 +217,60 @@
             take_far_above(k)
             take_far_below(k)
 
-    def spread(k, slots, job):
-        steps = PIECES // 2
-        t_per = tiles // steps if tiles >= steps else 1
-        which = k // steps
-        base = (k % steps) * t_per
-        for j in range(t_per):
-            job(slots(which), base + j)
+    group = 4 // PIECES
+
+    def near_tile(job):
+        slot = N1 - job // 2
+        if lines:
+            skip = ((z == 0) & (slot == P1)) | ((z == 3) & (slot == N1))
+            when(jnp.logical_not(skip), lambda: lane_tile(slot, job % 2))
+        else:
+            lane_tile(slot, job % 2)
 
     def second(k):
         far(k)
-        slot = N1 - k // (PIECES // 2)
-        t = k % (PIECES // 2)
-        if lines:
-            skip = ((z == 0) & (slot == P1)) | ((z == 3) & (slot == N1))
-            when(jnp.logical_not(skip), lambda: both_tiles(slot, t))
-        else:
-            both_tiles(slot, t)
+        for j in range(group):
+            near_tile(k * group + j)
 
     each(PIECES, second)
+
+    def far_tile(job):
+        slot = jnp.where(job == 2, N2 * core, N2 * job)
+        lane_tile(slot, job // 2)
 
     if lines:
         last = jnp.where(z == 0, P1, N1)
-
-    def third(k):
-        if lines:
+        half = rows // 2
+
+        def share_last(k):
+            return copy(held.at[mine + last], mine + last, k, send_sib.at[last], sibling)
+
+        def last_tile(h):
+            for j in range(PIECES // 2):
+                await_piece(other + last, h * (PIECES // 2) + j)
+            here = pl.ds(pl.multiple_of(h * half, half), half)
+            x = jnp.concatenate([held[mine + last, here, :], held[other + last, here, :]], axis=0)
+            one_tile(x, [limit(owner(last, core)), limit(owner(last, 1 - core))], h * half)
+
+        def third(q):
+            when(q < 3, lambda: far_tile(q))
+            when(ends & (q == 3), lambda: last_tile(q - 3))
+
             def take():
-                await_piece(mine + last, k)
-                share_last(k).start()
-
-            when(ends, take)
-        slot = N2 * (k // (PIECES // 2))
-        t = k % (PIECES // 2)
-        own_lane_tile(slot, t)
-
-    def share_last(k):
-        return copy(held.at[mine + last], mine + last, k, send_sib.at[last], sibling)
-
-    def far_other(t):
-        slot = N2 * core
-        other_lane_tile(slot, t)
-
-    each(tiles, far_other) if not lines else None
-    if lines:
-        def third_all(k):
-            third(k)
-            when((k % 2) == 0, lambda: far_other(k // 2))
-            when(ends & (k == PIECES - 1), lambda: both_tiles(last, 0))
-
-        each(PIECES, third_all)
-        when(ends, lambda: both_tiles(last, tiles - 1))
+                await_piece(mine + last, q // group)
+                share_last(q // group).start()
+
+            when(ends if group == 1 else ends & (q % 2 == 1), take)
+
+        each(4, third)
+        when(ends, lambda: last_tile(core * 0 + 1))
     else:
-        each(PIECES, third)
+        each(3, far_tile)
 
     total = jnp.sum(tot[...], axis=1, keepdims=True)
     count = counts_ref[me]
     valid = lax.broadcasted_iota(jnp.int32, (rows, 1), 0) < count
-    out_ref[...] = jnp.where(valid, acc[...] / total, 0.0).astype(out_ref.dtype)
+    out_ref[...] = jnp.where(valid, acc[...] * (1.0 / total), 0.0).astype(out_ref.dtype)
     across = jnp.transpose(jnp.broadcast_to(total, (rows, 128)))[0:1, :]
     dens_ref[...] = jnp.where(
         lax.broadcasted_iota(jnp.int32, (1, rows), 1) < count, across, 0.0)
@@ -321,16 +301,19 @@
             functools.partial(kernel, row_total, col_total),
             out_shape=(jax.ShapeDtypeStruct((1, rows), jnp.float32),
                        jax.ShapeDtypeStruct((rows, width), jnp.bfloat16)),
-            in_specs=[pl.BlockSpec(memory_space=pltpu.VMEM),
+            in_specs=[pl.BlockSpec(memory_space=pltpu.HBM),
                       pl.BlockSpec(memory_space=pltpu.SMEM),
-                      pl.BlockSpec(memory_space=pltpu.SMEM)],
+                      pl.BlockSpec(memory_space=pltpu.HBM)],
             out_specs=(pl.BlockSpec(memory_space=pltpu.VMEM),
                        pl.BlockSpec(memory_space=pltpu.VMEM)),
             scratch_shapes=[
+                pltpu.VMEM((rows, width), jnp.bfloat16),
+                pltpu.SMEM(pairs.shape, jnp.int32),
                 pltpu.VMEM((9, rows, width), jnp.bfloat16),
                 pltpu.VMEM((rows, width), jnp.float32),
                 pltpu.VMEM((rows, 128), jnp.float32),
-                pltpu.VMEM((rows, TILE), jnp.float32),
+                pltpu.VMEM((rows, rows), jnp.float32),
+                pltpu.SemaphoreType.DMA((2,)),
                 pltpu.SemaphoreType.DMA((3, PIECES)),
                 pltpu.SemaphoreType.DMA((4, PIECES)),
                 pltpu.SemaphoreType.DMA((4, PIECES)),

time: 70 us -> 65.7 us (0.939)
  Pallas kernels: 65.8 us -> 61.1 us
    pallas_call x1, Pallas kernels: 65.8 us -> 61.1 us  [body(): pl.pallas_call(functools.partial(kernel, row_total, col_total), out_shape...]
where the time goes in v2:
time: 65.7 us; the launch traced here: 65.1 us
  Pallas kernels  61.1 us (93%)
  local copies, waits for them, and re-layouts  3.37 us (5%)
    pallas_call x1, Pallas kernels, body(): pl.pallas_call(functools.partial(kernel, row_total, col_total), out_shape...  61.1 us
    unnamed x7, local copies, waits for them, and re-layouts  3.37 us

profile of v2, /device:TPU:0, one launch (start us, length us, event | category | flops | bytes accessed | tf_op | source)
XLA Modules:
  0.0 65.1 jit_solution(17091479004411255858)
XLA Ops:
  0.6 0.0 copy-start.1
  0.6 0.8 %copy.5.pairs_hbm = s32[32,6]{1,0:T(8,128)S(1)} copy(s32[32,6]{0,1:T(8,128)} %param.5) | data formatting | bytes 1536 | tf_op args[2]
  1.4 0.0 copy-done.1
  1.4 0.0 copy-start
  1.4 1.1 %copy-done = bf16[512,768]{1,0:T(8,128)(2,1)S(1)} copy-done((bf16[512,768]{1,0:T(8,128)(2,1)S(1)}, bf16[512,768]{1,0:T(8,128)(2,1)}, u32[]{:S(2)}) %copy-start) | copy-done | bytes 786456
  2.6 61.1 %shard_map.50 = (f32[1,512]{1,0:T(1,128)S(1)}, bf16[512,768]{1,0:T(8,128)(2,1)S(1)}) custom-call(bf16[512,768]{1,0:T(8,128)(2,1)S(1)} %copy-done, s32[32]{0:T(128)S(1)} %copy-done.1, s32[32,6]{1,0:T(8,128)S(1)} %copy.5.pairs_hbm), custom_call_target="tpu_custom_call" | custom-call | tf_op jit(solution)/shard_map/pallas_call | solution.py:300
  63.6 0.6 copy.8
  64.2 0.9 %copy.9 = bf16[512,768]{1,0:T(8,128)(2,1)} copy(bf16[512,768]{1,0:T(8,128)(2,1)S(1)} %get-tuple-element.9) | data formatting | bytes 1572864
Async XLA Ops:
  0.6 0.8 %copy-start.1 = (s32[32]{0:T(128)S(1)}, s32[32]{0:T(128)}, u32[]{:S(2)}) copy-start(s32[32]{0:T(128)} %counts_ref.1) | copy-start | bytes 388
  1.4 1.1 %copy-start = (bf16[512,768]{1,0:T(8,128)(2,1)S(1)}, bf16[512,768]{1,0:T(8,128)(2,1)}, u32[]{:S(2)}) copy-start(bf16[512,768]{1,0:T(8,128)(2,1)} %e_hbm.1) | copy-start | bytes 2359300
